TPU v7x, 128 devices: a whole 4x4x4 slice. The times are simulated.
128 devices in a mesh: tm: 16 (over x, z), batch: 8 (over y, core).
Axes of the slice: x: 4, y: 4, z: 4, core: 2. Of those that a mesh axis runs over, the one named last changes fastest.
Arguments:
- state: float32 [16, 8, 256, 1152], P('tm', 'batch'), may hold values from -6 to 6
- noise_draws: bfloat16 [2, 16, 8, 256, 1152], P(None, 'tm', 'batch'), may hold values from -6 to 6
- class_vec: float32 [8, 1152], P('batch'), may hold values from -6 to 6
- window_start: int32 [8], P('batch'), may hold values from 0 to 977
- advance: int32 [8], P('batch'), may hold values from 1 to 7
- step_dt: float32 [1000], replicated, may hold values from 0.05 to 0.2
- step_sigma: float32 [1000], replicated, may hold values from 0.05 to 0.2
- w_ada: bfloat16 [1152, 3456], replicated, may hold values from -0.1875 to 0.1875
- w_up: bfloat16 [4608, 1152], P(('tm', 'batch')), may hold values from -0.1875 to 0.1875
- w_down: bfloat16 [4608, 1152], P(('tm', 'batch')), may hold values from -0.09375 to 0.09375
Outputs:
- window_out: float32 [16, 8, 256, 1152], P('tm', 'batch')
All inputs are finite; a program needn't handle non-finite values.
Results may differ from a plain program's by a relative error of at most 0.0037.
Values may be sent and summed in bfloat16 or wider, within the bound.
No kernel may reach another device: no remote copies, remote signals or barrier semaphores. Data moves between devices by JAX's collectives and lax.ppermute only.
A program may use at most 128 MiB of HBM per device.

v0:
```python
import math
import jax
import jax.numpy as jnp
from jax import lax
from jax.sharding import PartitionSpec as P

SLIDE_BITS = 3
EPSILON = 1e-06


def spread_2(shard, axis, root):
    mine = lax.axis_index(axis) == root
    return lax.psum(jnp.where(mine, shard, jnp.zeros_like(shard)), axis)


def carried_in(part, axis, combine, identity):
    place = lax.axis_index(axis)
    gathered = lax.all_gather(part, axis)
    state = jnp.zeros_like(part) + jnp.asarray(identity, part.dtype)

    def one(turn, state):
        return combine(state, lax.dynamic_index_in_dim(gathered, turn, 0, False))

    return lax.fori_loop(0, place, one, state)


def from_behind(shard, axis, by):
    peers = lax.axis_size(axis)
    pairs = [(i, i + by) for i in range(peers) if 0 <= i + by < peers]
    return lax.ppermute(shard, axis, pairs)


def time_embed(steps_now, half_width):
    frequency = jnp.exp(-math.log(10000.0) * jnp.arange(half_width, dtype=jnp.float32) / half_width)
    angles = steps_now.astype(jnp.float32)[:, None] * frequency[None, :]
    return jnp.concatenate([jnp.cos(angles), jnp.sin(angles)], axis=1)


def dense_pair(hidden_rows, up_rows, down_rows):
    before = lax.dot_general(
        hidden_rows, up_rows, (((1,), (1,)), ((), ())), preferred_element_type=jnp.float32
    )
    activated = jax.nn.gelu(before, approximate=True).astype(jnp.bfloat16)
    return jnp.dot(activated, down_rows, preferred_element_type=jnp.float32)


def combine_sum(earlier, later):
    return earlier + later


def increment(current, noise_now, steps_now, class_vec, step_dt, step_sigma, w_ada, mlp_apply):
    images, tokens, channels = current.shape
    step_table = lax.iota(jnp.int32, step_dt.shape[0])
    onehot = (steps_now[:, None] == step_table[None, :]).astype(jnp.float32)
    step_size = jnp.sum(onehot * step_dt[None, :], axis=1)
    spread = jnp.sum(onehot * step_sigma[None, :], axis=1)
    condition = jax.nn.silu(time_embed(steps_now, channels // 2) + class_vec).astype(jnp.bfloat16)
    modulation = jnp.dot(condition, w_ada, preferred_element_type=jnp.float32)
    shift_by = modulation[:, :channels]
    scale_by = modulation[:, channels : 2 * channels]
    gate_by = modulation[:, 2 * channels :]
    mean_val = jnp.mean(current, axis=2, keepdims=True)
    centred = current - mean_val
    var_val = jnp.mean(centred * centred, axis=2, keepdims=True)
    normed = centred * lax.rsqrt(var_val + EPSILON)
    hidden_in = (normed * (1.0 + scale_by[:, None, :]) + shift_by[:, None, :]).astype(jnp.bfloat16)
    mlp_out = mlp_apply(hidden_in.reshape(images * tokens, channels)).reshape(
        images, tokens, channels
    )
    drift = gate_by[:, None, :] * mlp_out - current
    return step_size[:, None, None] * drift + spread[:, None, None] * noise_now.astype(jnp.float32)


def per_device(
    state, noise_draws, class_vec, window_start, advance, step_dt, step_sigma, w_ada, w_up, w_down
):
    window_size = lax.axis_size("tm")
    position = lax.axis_index("tm")
    up_whole, down_whole = (
        lax.all_gather(w_up, ("tm", "batch"), axis=0, tiled=True),
        lax.all_gather(w_down, ("tm", "batch"), axis=0, tiled=True),
    )

    def mlp_apply(hidden_rows):
        return dense_pair(hidden_rows, up_whole, down_whole)

    def sweep(current, noise_now, starts):
        steps_now = starts + position
        step_inc = increment(
            current, noise_now, steps_now, class_vec, step_dt, step_sigma, w_ada, mlp_apply
        )
        base_rows = spread_2(current, "tm", 0)
        prefix = carried_in(step_inc, "tm", combine_sum, jnp.zeros_like(step_inc))
        updated = base_rows + prefix
        return (updated, step_inc)

    updated, step_inc = sweep(state[0], noise_draws[0, 0], window_start)
    end_rows = updated + step_inc
    tail_rows = jnp.where(position == window_size - 1, end_rows, jnp.zeros_like(end_rows))
    moved = updated
    for section_bit in range(SLIDE_BITS):
        distance = 1 << section_bit
        arrived, arrived_tail = from_behind((moved, tail_rows), "tm", -distance)
        taken = advance >> section_bit & 1 == 1
        outside = position + distance >= window_size
        incoming = jnp.where(outside, tail_rows, arrived)
        moved = jnp.where(taken[:, None, None], incoming, moved)
        tail_rows = jnp.where(position >= window_size - distance, tail_rows, arrived_tail)
    final_rows, leftover = sweep(moved, noise_draws[1, 0], window_start + advance)
    return final_rows[None]


def solution(mesh):
    in_specs = (
        P("tm", "batch", None, None),
        P(None, "tm", "batch", None, None),
        P("batch", None),
        P("batch"),
        P("batch"),
        P(),
        P(),
        P(),
        P(("tm", "batch"), None),
        P(("tm", "batch"), None),
    )
    out_specs = P("tm", "batch", None, None)
    return jax.shard_map(
        per_device, mesh=mesh, in_specs=in_specs, out_specs=out_specs, check_vma=False
    )
```

profile of v0, /device:TPU:0, one launch (start us, length us, event | category | flops | bytes accessed | tf_op | source)
XLA Modules:
  0.0 791.6 jit_solution(7158159004411722302)
XLA Ops:
  9.4 1.4 reduce_sum.73
  11.6 4.5 fusion.73
  16.2 1.2 fusion.39
  17.4 68.0 %all-gather.15.cloned.1.call-done = bf16[128,36,1152]{2,1,0:T(8,128)(2,1)} async-done(((bf16[1,36,1152]{2,1,0:T(8,128)(2,1)}), bf16[128,36,1152]{2,1,0:T(8,128)(2,1)}) %all-gather.15.cloned.1.call-update) | async-done | bytes 10616848 | tf_op jit(solution)/shard_map/all_gather | solution.py:81
  85.3 16.3 %reshape.304 = bf16[4608,1152]{1,0:T(8,128)(2,1)} reshape(bf16[128,36,1152]{2,1,0:T(8,128)(2,1)} %all-gather.15.cloned.1.call-done) | data formatting | bytes 21233664
  101.6 58.2 %all-gather.13.cloned.1.call-done = bf16[128,36,1152]{2,1,0:T(8,128)(2,1)} async-done(((bf16[1,36,1152]{2,1,0:T(8,128)(2,1)}), bf16[128,36,1152]{2,1,0:T(8,128)(2,1)}) %all-gather.13.cloned.1.call-update) | async-done | bytes 10616848 | tf_op jit(solution)/shard_map/all_gather | solution.py:80
  159.9 16.3 %reshape.302 = bf16[4608,1152]{1,0:T(8,128)(2,1)} reshape(bf16[128,36,1152]{2,1,0:T(8,128)(2,1)} %all-gather.13.cloned.1.call-done) | data formatting | bytes 21233664
  176.2 15.8 %fusion.18 = f32[256,1152]{1,0:T(8,128)} fusion(bf16[4608,1152]{1,0:T(8,128)(2,1)} %reshape.304, f32[1,1,256,1152]{3,2,1,0:T(8,128)S(1)} %copy-done.1, bf16[4608,1152]{1,0:T(8,128)(2,1)} %reshape.302, bf16[2,1,1,256,1152]{4,3,2,1,0:T(8,128)(2,1)S(1)} %copy-done.10, f32[]{:T(128)} %get-tuple-element.86, f32[1152]{0:T(1024)S(1)} %get-tuple-element.82, ...), kind=kOutput, calls=%fused_computation.24 | convolution fusion | flops 5449678848 | bytes 25389064 | tf_op jit(solution)/shard_map/dot_general | solution.py:44
  192.6 120.7 %all-gather.9.cloned.1.call-done = f32[4096,1152]{1,0:T(8,128)} async-done(((f32[256,1152]{1,0:T(8,128)}), f32[4096,1152]{1,0:T(8,128)}) %all-gather.9.cloned.1.call-update) | async-done | bytes 18874384 | tf_op jit(solution)/shard_map/all_gather | solution.py:18
  313.4 89.8 %all-reduce.3.cloned.1.call-done = f32[1,256,1152]{2,1,0:T(8,128)} async-done(((f32[1,256,1152]{2,1,0:T(8,128)}), f32[1,256,1152]{2,1,0:T(8,128)}) %all-reduce.3.cloned.1.call-update) | async-done | bytes 1179664 | tf_op jit(solution)/shard_map/psum | solution.py:13
  403.2 1.5 add.160
  404.7 1.3 collective-permute-start.2
  406.0 26.8 %collective-permute-done.2 = f32[1,256,1152]{2,1,0:T(8,128)S(1)} collective-permute-done((f32[1,256,1152]{2,1,0:T(8,128)S(1)}, f32[1,256,1152]{2,1,0:T(8,128)S(1)}, u32[]{:S(2)}, u32[]{:S(2)}) %collective-permute-start.2) | collective-permute-done | bytes 1179680 | tf_op jit(solution)/shard_map/ppermute | solution.py:30
  432.8 1.0 copy-done.2
  433.9 2.5 select_select_fusion.2
  436.3 1.3 collective-permute-start.3
  437.6 1.3 collective-permute-start
  438.9 26.1 %collective-permute-done.3 = f32[1,256,1152]{2,1,0:T(8,128)S(1)} collective-permute-done((f32[1,256,1152]{2,1,0:T(8,128)S(1)}, f32[1,256,1152]{2,1,0:T(8,128)S(1)}, u32[]{:S(2)}, u32[]{:S(2)}) %collective-permute-start.3) | collective-permute-done | bytes 1179680 | tf_op jit(solution)/shard_map/ppermute | solution.py:30
  465.0 25.3 %collective-permute-done = f32[1,256,1152]{2,1,0:T(8,128)S(1)} collective-permute-done((f32[1,256,1152]{2,1,0:T(8,128)}, f32[1,256,1152]{2,1,0:T(8,128)S(1)}, u32[]{:S(2)}, u32[]{:S(2)}) %collective-permute-start) | collective-permute-done | bytes 1179680 | tf_op jit(solution)/shard_map/ppermute | solution.py:30
  490.3 1.0 copy-done.5
  491.4 1.9 select_select_fusion.1
  493.2 1.3 collective-permute-start.4
  494.5 1.5 collective-permute-start.1
  496.1 4.4 fusion.71
  501.2 22.9 %collective-permute-done.4 = f32[1,256,1152]{2,1,0:T(8,128)S(1)} collective-permute-done((f32[1,256,1152]{2,1,0:T(8,128)S(1)}, f32[1,256,1152]{2,1,0:T(8,128)S(1)}, u32[]{:S(2)}, u32[]{:S(2)}) %collective-permute-start.4) | collective-permute-done | bytes 1179680 | tf_op jit(solution)/shard_map/ppermute | solution.py:30
  524.1 0.7 collective-permute-done.1
  525.1 1.9 fusion.101
  527.0 1.2 multiply_reduce_fusion
  528.6 15.9 %fusion.22 = f32[1,256,1152]{2,1,0:T(8,128)} fusion(f32[1,256,1152]{2,1,0:T(8,128)S(1)} %get-tuple-element.104, bf16[4608,1152]{1,0:T(8,128)(2,1)} %reshape.304, bf16[4608,1152]{1,0:T(8,128)(2,1)} %reshape.302, bf16[2,1,1,256,1152]{4,3,2,1,0:T(8,128)(2,1)S(1)} %copy-done.11, f32[]{:T(128)} %get-tuple-element.85, f32[1152]{0:T(1024)S(1)} %copy-done.7, ...), kind=kOutput, calls=%fused_computation.28 | convolution fusion | flops 5449678848 | bytes 25389064 | tf_op jit(solution)/shard_map/dot_general | solution.py:44
  545.1 147.3 %all-gather.11.cloned.1.call-done = f32[16,256,1152]{2,1,0:T(8,128)} async-done(((f32[1,256,1152]{2,1,0:T(8,128)}), f32[16,256,1152]{2,1,0:T(8,128)}) %all-gather.11.cloned.1.call-update) | async-done | bytes 18874384 | tf_op jit(solution)/shard_map/all_gather | solution.py:18
  692.5 89.8 %all-reduce.5.cloned.1.call-done = f32[1,256,1152]{2,1,0:T(8,128)} async-done(((f32[1,256,1152]{2,1,0:T(8,128)}), f32[1,256,1152]{2,1,0:T(8,128)}) %all-reduce.5.cloned.1.call-update) | async-done | bytes 1179664 | tf_op jit(solution)/shard_map/psum | solution.py:13
  782.3 2.4 add_bitcast_fusion
  (47 shorter events, 5.1 us)
Async XLA Ops:
  6.5 4.3 copy-start.8
  6.5 4.3 copy-start.9
  6.5 5.0 copy-start.6
  6.5 78.8 %all-gather.15.cloned.1.call-start = ((), (), s32[]{:S(2)}) async-start(), calls=%async_computation.5 | async-start | bytes 11888640 | tf_op jit(solution)/shard_map/all_gather | solution.py:81
  7.3 152.6 %all-gather.13.cloned.1.call-start = ((), (), s32[]{:S(2)}) async-start(), calls=%async_computation.4 | async-start | bytes 11888640 | tf_op jit(solution)/shard_map/all_gather | solution.py:80
  8.0 305.3 %all-gather.9.cloned.1.call-start = ((), (), s32[]{:S(2)}) async-start(), calls=%async_computation.2 | async-start | bytes 20054016 | tf_op jit(solution)/shard_map/all_gather | solution.py:18
  11.6 4.6 copy-start.1
  101.6 74.6 %copy-start.10 = (bf16[2,1,1,256,1152]{4,3,2,1,0:T(8,128)(2,1)S(1)}, bf16[2,1,1,256,1152]{4,3,2,1,0:T(8,128)(2,1)}, u32[]{:S(2)}) copy-start(bf16[2,1,1,256,1152]{4,3,2,1,0:T(8,128)(2,1)} %param.15) | copy-start | bytes 3538948
  192.0 211.2 %all-reduce.3.cloned.1.call-start = ((), (), s32[]{:S(2)}) async-start(), calls=%async_computation | async-start | bytes 2359296 | tf_op jit(solution)/shard_map/psum | solution.py:13
  192.6 499.8 %all-gather.11.cloned.1.call-start = ((), (), s32[]{:S(2)}) async-start(), calls=%async_computation.3 | async-start | bytes 20054016 | tf_op jit(solution)/shard_map/all_gather | solution.py:18
  403.2 30.6 %copy-start = (f32[256,1152]{1,0:T(8,128)S(1)}, f32[256,1152]{1,0:T(8,128)}, u32[]{:S(2)}) copy-start(f32[256,1152]{1,0:T(8,128)} %fusion.18) | copy-start | bytes 3538948
  404.7 28.1 %collective-permute-start.2 = (f32[1,256,1152]{2,1,0:T(8,128)S(1)}, f32[1,256,1152]{2,1,0:T(8,128)S(1)}, u32[]{:S(2)}, u32[]{:S(2)}) collective-permute-start(f32[1,256,1152]{2,1,0:T(8,128)S(1)} %add.160), channel_id=1, source_target_pairs={{8,0},{16,8},{24,16},{32,24},{40,32},{48,40},{56,48},{64,56},{72,6... | collective-permute-start | bytes 3538952 | tf_op jit(solution)/shard_map/ppermute | solution.py:30
  432.8 1.0 copy-start.2
  436.3 28.7 %collective-permute-start.3 = (f32[1,256,1152]{2,1,0:T(8,128)S(1)}, f32[1,256,1152]{2,1,0:T(8,128)S(1)}, u32[]{:S(2)}, u32[]{:S(2)}) collective-permute-start(f32[1,256,1152]{2,1,0:T(8,128)S(1)} %get-tuple-element.107), channel_id=1, source_target_pairs={{16,0},{24,8},{32,16},{40,24},{48,32},{56,40},{64,48},{72,56},{80,... | collective-permute-start | bytes 3538952 | tf_op jit(solution)/shard_map/ppermute | solution.py:30
  437.6 52.7 %collective-permute-start = (f32[1,256,1152]{2,1,0:T(8,128)}, f32[1,256,1152]{2,1,0:T(8,128)S(1)}, u32[]{:S(2)}, u32[]{:S(2)}) collective-permute-start(f32[1,256,1152]{2,1,0:T(8,128)} %get-tuple-element.108), channel_id=1, source_target_pairs={{8,0},{16,8},{24,16},{32,24},{40,32},{48,40},{56,48},{64,56},{72,6... | collective-permute-start | bytes 3538952 | tf_op jit(solution)/shard_map/ppermute | solution.py:30
  465.0 25.3 %copy-start.4 = (f32[1,256,1152]{2,1,0:T(8,128)}, f32[1,256,1152]{2,1,0:T(8,128)S(1)}, u32[]{:S(2)}) copy-start(f32[1,256,1152]{2,1,0:T(8,128)S(1)} %collective-permute-done.3) | copy-start | bytes 3538948
  490.3 1.1 copy-start.5
  493.2 30.8 %collective-permute-start.4 = (f32[1,256,1152]{2,1,0:T(8,128)S(1)}, f32[1,256,1152]{2,1,0:T(8,128)S(1)}, u32[]{:S(2)}, u32[]{:S(2)}) collective-permute-start(f32[1,256,1152]{2,1,0:T(8,128)S(1)} %get-tuple-element.105), channel_id=1, source_target_pairs={{32,0},{40,8},{48,16},{56,24},{64,32},{72,40},{80,48},{88,56},{96,... | collective-permute-start | bytes 3538952 | tf_op jit(solution)/shard_map/ppermute | solution.py:30
  494.5 30.3 %collective-permute-start.1 = (f32[1,256,1152]{2,1,0:T(8,128)S(1)}, f32[1,256,1152]{2,1,0:T(8,128)}, u32[]{:S(2)}, u32[]{:S(2)}) collective-permute-start(f32[1,256,1152]{2,1,0:T(8,128)S(1)} %get-tuple-element.106), channel_id=1, source_target_pairs={{16,0},{24,8},{32,16},{40,24},{48,32},{56,40},{64,48},{72,56},{80,... | collective-permute-start | bytes 3538952 | tf_op jit(solution)/shard_map/ppermute | solution.py:30
  524.1 1.0 copy-start.3
  527.0 1.2 copy-start.7
  527.0 1.6 copy-start.11
  544.5 237.8 %all-reduce.5.cloned.1.call-start = ((), (), s32[]{:S(2)}) async-start(), calls=%async_computation.1 | async-start | bytes 2359296 | tf_op jit(solution)/shard_map/psum | solution.py:13
Sparse Core Ops, SparseCore 0:
  10.3 74.9 all-gather.14
  88.3 71.5 all-gather.12
  192.1 121.1 all-gather.8
  316.5 86.6 all-reduce.2
  544.6 147.7 all-gather.10
  695.6 86.6 all-reduce.4
where the time goes:
time: 794 us; the launch traced here: 792 us
  waiting for transfers between devices  678 us (85%)
  matrix products  40.6 us (5%)
  local copies, waits for them, and re-layouts  35.5 us (4%)
  other arithmetic  15.6 us (2%)
  between operations  15 us (2%)
    all_gather x2, waiting for transfers between devices, carried_in(): gathered = lax.all_gather(part, axis)  268 us
    psum x2, waiting for transfers between devices, spread_2(): return lax.psum(jnp.where(mine, shard, jnp.zeros_like(shard)), axis)  180 us
    ppermute x5, waiting for transfers between devices, from_behind(): return lax.ppermute(shard, axis, pairs)  102 us
    all_gather x1, waiting for transfers between devices, per_device(): lax.all_gather(w_down, ('tm', 'batch'), axis=0, tiled=True)  68 us
    all_gather x1, waiting for transfers between devices, per_device(): lax.all_gather(w_up, ('tm', 'batch'), axis=0, tiled=True)  58.2 us
    unnamed x26, local copies, waits for them, and re-layouts  35.3 us
    dot_general x2, matrix products, dense_pair(): return jnp.dot(activated, down_rows, preferred_element_type=jnp.float32)  31.7 us
  transfers between devices with their start and end apart: 11, of which 11 were waited for; matrix products, arithmetic and copies ran while one was open for 4% of the time, Pallas kernels for 0%

commit v1 on v0

--- a/solution.py
+++ b/solution.py
@@ -77,7 +77,12 @@
     window_size = lax.axis_size("tm")
     position = lax.axis_index("tm")
     up_whole, down_whole = (
-        lax.all_gather(w_up, ("tm", "batch"), axis=0, tiled=True),
+        jnp.concatenate(
+            lax.all_to_all(
+                jnp.stack([w_up] * lax.axis_size(("tm", "batch"))), ("tm", "batch"), 0, 0
+            ),
+            axis=0,
+        ),
         lax.all_gather(w_down, ("tm", "batch"), axis=0, tiled=True),
     )
 

time: 794 us -> 840 us (1.058)
  waiting for transfers between devices: 678 us -> 708 us
  starting transfers between devices: 6.83 us -> 18.4 us
    all_to_all x0 -> x1, waiting for transfers between devices: none -> 151 us  [per_device(): lax.all_to_all(jnp.stack([w_up] * lax.axis_size(('tm', 'batch'))), ('tm',...]
    all_gather x1, waiting for transfers between devices: 68 us -> 5.74 us  [per_device(): lax.all_gather(w_down, ('tm', 'batch'), axis=0, tiled=True)]
    all_gather x1 -> x0, waiting for transfers between devices: 58.2 us -> none  [per_device(): lax.all_gather(w_up, ('tm', 'batch'), axis=0, tiled=True)]
    reshape x0 -> x1, local copies, waits for them, and re-layouts: none -> 16.6 us  [per_device(): jnp.concatenate(lax.all_to_all(jnp.stack([w_up] * lax.axis_size(('tm', 'b...]
    unnamed x26 -> x25, local copies, waits for them, and re-layouts: 35.3 us -> 19.1 us
    all_to_all x0 -> x1, starting transfers between devices: none -> 11.6 us  [per_device(): lax.all_to_all(jnp.stack([w_up] * lax.axis_size(('tm', 'batch'))), ('tm',...]
where the time goes in v1:
time: 840 us; the launch traced here: 837 us
  waiting for transfers between devices  708 us (84%)
  local copies, waits for them, and re-layouts  41.8 us (5%)
  matrix products  40.5 us (5%)
  starting transfers between devices  18.4 us (2%)
  between operations  14.7 us (2%)
  other arithmetic  14.3 us (2%)
    all_gather x2, waiting for transfers between devices, carried_in(): gathered = lax.all_gather(part, axis)  268 us
    psum x2, waiting for transfers between devices, spread_2(): return lax.psum(jnp.where(mine, shard, jnp.zeros_like(shard)), axis)  180 us
    all_to_all x1, waiting for transfers between devices, per_device(): lax.all_to_all(jnp.stack([w_up] * lax.axis_size(('tm', 'batch'))), ('tm',...  151 us
    ppermute x5, waiting for transfers between devices, from_behind(): return lax.ppermute(shard, axis, pairs)  102 us
    dot_general x2, matrix products, dense_pair(): return jnp.dot(activated, down_rows, preferred_element_type=jnp.float32)  31.7 us
    unnamed x25, local copies, waits for them, and re-layouts  19.1 us
  transfers between devices with their start and end apart: 11, of which 11 were waited for; matrix products, arithmetic and copies ran while one was open for 4% of the time, Pallas kernels for 0%

profile of v1, /device:TPU:0, one launch (start us, length us, event | category | flops | bytes accessed | tf_op | source)
XLA Modules:
  0.0 837.3 jit_solution(16758103040733630025)
XLA Ops:
  7.3 6.0 stack.2
  13.2 11.6 %all-to-all-start = ((bf16[128,36,1152]{2,1,0:T(8,128)(2,1)}), bf16[128,36,1152]{2,1,0:T(8,128)(2,1)}, u32[]{:S(2)}, u32[]{:S(2)}) async-start(bf16[128,36,1152]{2,1,0:T(8,128)(2,1)} %stack.2), calls=%async_computation | async-start | bytes 23592960 | tf_op jit(solution)/shard_map/all_to_all | solution.py:81
  27.2 4.4 fusion.70
  31.7 1.2 fusion.35
  32.9 150.6 %all-to-all-done = bf16[128,36,1152]{2,1,0:T(8,128)(2,1)} async-done(((bf16[128,36,1152]{2,1,0:T(8,128)(2,1)}), bf16[128,36,1152]{2,1,0:T(8,128)(2,1)}, u32[]{:S(2)}, u32[]{:S(2)}) %all-to-all-start) | async-done | bytes 10616864 | tf_op jit(solution)/shard_map/all_to_all | solution.py:81
  183.5 16.6 %reshape.323 = bf16[4608,1152]{1,0:T(8,128)(2,1)} reshape(bf16[128,36,1152]{2,1,0:T(8,128)(2,1)} %all-to-all-done) | data formatting | bytes 21233664 | tf_op jit(solution)/shard_map/reshape | solution.py:80
  200.1 5.7 all-gather.11.cloned.1.call-done
  205.8 16.3 %reshape.329 = bf16[4608,1152]{1,0:T(8,128)(2,1)} reshape(bf16[128,36,1152]{2,1,0:T(8,128)(2,1)} %all-gather.11.cloned.1.call-done) | data formatting | bytes 21233664
  222.1 15.8 %fusion.18 = f32[256,1152]{1,0:T(8,128)} fusion(bf16[4608,1152]{1,0:T(8,128)(2,1)} %reshape.329, f32[1,1,256,1152]{3,2,1,0:T(8,128)S(1)} %copy-done.1, bf16[4608,1152]{1,0:T(8,128)(2,1)} %reshape.323, bf16[2,1,1,256,1152]{4,3,2,1,0:T(8,128)(2,1)S(1)} %copy-done.10, f32[]{:T(128)} %get-tuple-element.86, f32[1152]{0:T(1024)S(1)} %get-tuple-element.82, ...), kind=kOutput, calls=%fused_computation.24 | convolution fusion | flops 5449678848 | bytes 25389064 | tf_op jit(solution)/shard_map/dot_general | solution.py:44
  238.8 120.5 %all-gather.7.cloned.1.call-done = f32[4096,1152]{1,0:T(8,128)} async-done(((f32[256,1152]{1,0:T(8,128)}), f32[4096,1152]{1,0:T(8,128)}) %all-gather.7.cloned.1.call-update) | async-done | bytes 18874384 | tf_op jit(solution)/shard_map/all_gather | solution.py:18
  359.4 89.9 %all-reduce.3.cloned.1.call-done = f32[1,256,1152]{2,1,0:T(8,128)} async-done(((f32[1,256,1152]{2,1,0:T(8,128)}), f32[1,256,1152]{2,1,0:T(8,128)}) %all-reduce.3.cloned.1.call-update) | async-done | bytes 1179664 | tf_op jit(solution)/shard_map/psum | solution.py:13
  449.3 1.5 add.165
  450.8 1.3 collective-permute-start.2
  452.1 26.8 %collective-permute-done.2 = f32[1,256,1152]{2,1,0:T(8,128)S(1)} collective-permute-done((f32[1,256,1152]{2,1,0:T(8,128)S(1)}, f32[1,256,1152]{2,1,0:T(8,128)S(1)}, u32[]{:S(2)}, u32[]{:S(2)}) %collective-permute-start.2) | collective-permute-done | bytes 1179680 | tf_op jit(solution)/shard_map/ppermute | solution.py:30
  479.0 1.0 copy-done.2
  480.0 2.5 select_select_fusion.2
  482.4 1.3 collective-permute-start.3
  483.7 1.3 collective-permute-start
  485.0 26.1 %collective-permute-done.3 = f32[1,256,1152]{2,1,0:T(8,128)S(1)} collective-permute-done((f32[1,256,1152]{2,1,0:T(8,128)S(1)}, f32[1,256,1152]{2,1,0:T(8,128)S(1)}, u32[]{:S(2)}, u32[]{:S(2)}) %collective-permute-start.3) | collective-permute-done | bytes 1179680 | tf_op jit(solution)/shard_map/ppermute | solution.py:30
  511.1 25.3 %collective-permute-done = f32[1,256,1152]{2,1,0:T(8,128)S(1)} collective-permute-done((f32[1,256,1152]{2,1,0:T(8,128)}, f32[1,256,1152]{2,1,0:T(8,128)S(1)}, u32[]{:S(2)}, u32[]{:S(2)}) %collective-permute-start) | collective-permute-done | bytes 1179680 | tf_op jit(solution)/shard_map/ppermute | solution.py:30
  536.4 1.0 copy-done.5
  537.5 1.9 select_select_fusion.1
  539.3 1.3 collective-permute-start.4
  540.6 1.5 collective-permute-start.1
  542.2 4.4 fusion.68
  547.3 22.9 %collective-permute-done.4 = f32[1,256,1152]{2,1,0:T(8,128)S(1)} collective-permute-done((f32[1,256,1152]{2,1,0:T(8,128)S(1)}, f32[1,256,1152]{2,1,0:T(8,128)S(1)}, u32[]{:S(2)}, u32[]{:S(2)}) %collective-permute-start.4) | collective-permute-done | bytes 1179680 | tf_op jit(solution)/shard_map/ppermute | solution.py:30
  571.2 1.9 fusion.98
  573.1 1.2 multiply_reduce_fusion
  574.7 15.9 %fusion.22 = f32[1,256,1152]{2,1,0:T(8,128)} fusion(f32[1,256,1152]{2,1,0:T(8,128)S(1)} %get-tuple-element.104, bf16[4608,1152]{1,0:T(8,128)(2,1)} %reshape.329, bf16[4608,1152]{1,0:T(8,128)(2,1)} %reshape.323, bf16[2,1,1,256,1152]{4,3,2,1,0:T(8,128)(2,1)S(1)} %copy-done.11, f32[]{:T(128)} %get-tuple-element.85, f32[1152]{0:T(1024)S(1)} %copy-done.7, ...), kind=kOutput, calls=%fused_computation.28 | convolution fusion | flops 5449678848 | bytes 25389064 | tf_op jit(solution)/shard_map/dot_general | solution.py:44
  591.2 147.3 %all-gather.9.cloned.1.call-done = f32[16,256,1152]{2,1,0:T(8,128)} async-done(((f32[1,256,1152]{2,1,0:T(8,128)}), f32[16,256,1152]{2,1,0:T(8,128)}) %all-gather.9.cloned.1.call-update) | async-done | bytes 18874384 | tf_op jit(solution)/shard_map/all_gather | solution.py:18
  738.6 89.8 %all-reduce.5.cloned.1.call-done = f32[1,256,1152]{2,1,0:T(8,128)} async-done(((f32[1,256,1152]{2,1,0:T(8,128)}), f32[1,256,1152]{2,1,0:T(8,128)}) %all-reduce.5.cloned.1.call-update) | async-done | bytes 1179664 | tf_op jit(solution)/shard_map/psum | solution.py:13
  828.4 2.4 add_bitcast_fusion
  (47 shorter events, 5.5 us)
Async XLA Ops:
  6.5 199.3 %all-gather.11.cloned.1.call-start = ((), (), s32[]{:S(2)}) async-start(), calls=%async_computation.5 | async-start | bytes 11888640 | tf_op jit(solution)/shard_map/all_gather | solution.py:86
  13.2 13.0 %copy-start.1 = (f32[1,1,256,1152]{3,2,1,0:T(8,128)S(1)}, f32[1,1,256,1152]{3,2,1,0:T(8,128)}, u32[]{:S(2)}) copy-start(f32[1,1,256,1152]{3,2,1,0:T(8,128)} %param.14) | copy-start | bytes 3538948
  13.2 170.3 %all-to-all-start = ((bf16[128,36,1152]{2,1,0:T(8,128)(2,1)}), bf16[128,36,1152]{2,1,0:T(8,128)(2,1)}, u32[]{:S(2)}, u32[]{:S(2)}) async-start(bf16[128,36,1152]{2,1,0:T(8,128)(2,1)} %stack.2), calls=%async_computation | async-start | bytes 23592960 | tf_op jit(solution)/shard_map/all_to_all | solution.py:81
  24.9 1.6 copy-start.8
  24.9 1.6 copy-start.9
  24.9 2.3 copy-start.6
  24.9 334.4 %all-gather.7.cloned.1.call-start = ((), (), s32[]{:S(2)}) async-start(), calls=%async_computation.3 | async-start | bytes 20054016 | tf_op jit(solution)/shard_map/all_gather | solution.py:18
  200.1 22.0 %copy-start.10 = (bf16[2,1,1,256,1152]{4,3,2,1,0:T(8,128)(2,1)S(1)}, bf16[2,1,1,256,1152]{4,3,2,1,0:T(8,128)(2,1)}, u32[]{:S(2)}) copy-start(bf16[2,1,1,256,1152]{4,3,2,1,0:T(8,128)(2,1)} %param.15) | copy-start | bytes 3538948
  238.0 211.4 %all-reduce.3.cloned.1.call-start = ((), (), s32[]{:S(2)}) async-start(), calls=%async_computation.1 | async-start | bytes 2359296 | tf_op jit(solution)/shard_map/psum | solution.py:13
  238.7 499.8 %all-gather.9.cloned.1.call-start = ((), (), s32[]{:S(2)}) async-start(), calls=%async_computation.4 | async-start | bytes 20054016 | tf_op jit(solution)/shard_map/all_gather | solution.py:18
  449.3 30.6 %copy-start = (f32[256,1152]{1,0:T(8,128)S(1)}, f32[256,1152]{1,0:T(8,128)}, u32[]{:S(2)}) copy-start(f32[256,1152]{1,0:T(8,128)} %fusion.18) | copy-start | bytes 3538948
  450.8 28.1 %collective-permute-start.2 = (f32[1,256,1152]{2,1,0:T(8,128)S(1)}, f32[1,256,1152]{2,1,0:T(8,128)S(1)}, u32[]{:S(2)}, u32[]{:S(2)}) collective-permute-start(f32[1,256,1152]{2,1,0:T(8,128)S(1)} %add.165), channel_id=1, source_target_pairs={{8,0},{16,8},{24,16},{32,24},{40,32},{48,40},{56,48},{64,56},{72,6... | collective-permute-start | bytes 3538952 | tf_op jit(solution)/shard_map/ppermute | solution.py:30
  478.9 1.0 copy-start.2
  482.4 28.7 %collective-permute-start.3 = (f32[1,256,1152]{2,1,0:T(8,128)S(1)}, f32[1,256,1152]{2,1,0:T(8,128)S(1)}, u32[]{:S(2)}, u32[]{:S(2)}) collective-permute-start(f32[1,256,1152]{2,1,0:T(8,128)S(1)} %get-tuple-element.107), channel_id=1, source_target_pairs={{16,0},{24,8},{32,16},{40,24},{48,32},{56,40},{64,48},{72,56},{80,... | collective-permute-start | bytes 3538952 | tf_op jit(solution)/shard_map/ppermute | solution.py:30
  483.7 52.7 %collective-permute-start = (f32[1,256,1152]{2,1,0:T(8,128)}, f32[1,256,1152]{2,1,0:T(8,128)S(1)}, u32[]{:S(2)}, u32[]{:S(2)}) collective-permute-start(f32[1,256,1152]{2,1,0:T(8,128)} %get-tuple-element.108), channel_id=1, source_target_pairs={{8,0},{16,8},{24,16},{32,24},{40,32},{48,40},{56,48},{64,56},{72,6... | collective-permute-start | bytes 3538952 | tf_op jit(solution)/shard_map/ppermute | solution.py:30
  511.1 25.3 %copy-start.4 = (f32[1,256,1152]{2,1,0:T(8,128)}, f32[1,256,1152]{2,1,0:T(8,128)S(1)}, u32[]{:S(2)}) copy-start(f32[1,256,1152]{2,1,0:T(8,128)S(1)} %collective-permute-done.3) | copy-start | bytes 3538948
  536.4 1.1 copy-start.5
  539.3 30.8 %collective-permute-start.4 = (f32[1,256,1152]{2,1,0:T(8,128)S(1)}, f32[1,256,1152]{2,1,0:T(8,128)S(1)}, u32[]{:S(2)}, u32[]{:S(2)}) collective-permute-start(f32[1,256,1152]{2,1,0:T(8,128)S(1)} %get-tuple-element.105), channel_id=1, source_target_pairs={{32,0},{40,8},{48,16},{56,24},{64,32},{72,40},{80,48},{88,56},{96,... | collective-permute-start | bytes 3538952 | tf_op jit(solution)/shard_map/ppermute | solution.py:30
  540.6 30.3 %collective-permute-start.1 = (f32[1,256,1152]{2,1,0:T(8,128)S(1)}, f32[1,256,1152]{2,1,0:T(8,128)}, u32[]{:S(2)}, u32[]{:S(2)}) collective-permute-start(f32[1,256,1152]{2,1,0:T(8,128)S(1)} %get-tuple-element.106), channel_id=1, source_target_pairs={{16,0},{24,8},{32,16},{40,24},{48,32},{56,40},{64,48},{72,56},{80,... | collective-permute-start | bytes 3538952 | tf_op jit(solution)/shard_map/ppermute | solution.py:30
  570.2 1.0 copy-start.3
  573.1 1.2 copy-start.7
  573.1 1.6 copy-start.11
  590.6 237.8 %all-reduce.5.cloned.1.call-start = ((), (), s32[]{:S(2)}) async-start(), calls=%async_computation.2 | async-start | bytes 2359296 | tf_op jit(solution)/shard_map/psum | solution.py:13
Sparse Core Ops, SparseCore 0:
  10.3 195.4 all-gather.10
  238.1 121.1 all-gather.6
  362.6 86.6 all-reduce.2
  590.8 147.7 all-gather.8
  741.7 86.6 all-reduce.4
